TPU v7x, 512 devices: a whole 4x8x8 slice. The times are simulated.
512 devices in a mesh: leaf: 64 (over x, y, core), grp: 8 (over z).
Axes of the slice: x: 4, y: 8, z: 8, core: 2. Of those that a mesh axis runs over, the one named last changes fastest.
Arguments:
- signal: bfloat16 [64, 2097152], P(None, ('leaf', 'grp')), may hold values from -6 to 6
- points: bfloat16 [3, 2097152], P(None, ('leaf', 'grp')), may hold values from 0 to 1
- basis: bfloat16 [4096, 512, 128], P(('leaf', 'grp')), may hold values from -0.25 to 0.25
- transfer: bfloat16 [4096, 128, 128], P(('leaf', 'grp')), may hold values from -0.5 to 0.5
- leaf_src: int32 [4096, 8], P(('leaf', 'grp')), may hold values from 0 to 63, as said below
- leaf_count: int32 [4096], P(('leaf', 'grp')), may hold values from 1 to 8, as said below
- leaf_blocks: bfloat16 [4096, 8, 128, 128], P(('leaf', 'grp')), may hold values from -0.25 to 0.25
- cluster_src: int32 [64, 16], P('leaf', 'grp'), may hold values from 0 to 63, as said below
- cluster_count: int32 [64], P('leaf'), may hold values from 1 to 16, as said below
- cluster_blocks: bfloat16 [64, 16, 128, 128], P('leaf', 'grp'), may hold values from -0.03125 to 0.03125
Outputs:
- output: bfloat16 [64, 2097152], P(None, ('leaf', 'grp'))
Inputs may be any that keep to these rules, and one draw needn't show every extreme that they name: `leaf_src`: each row holds distinct leaves; for leaf number a within its cluster every entry differs from a by 3 to 64 - 3 modulo 64. Slots at or beyond leaf_count hold valid numbers that are not used. `leaf_count`: some leaf uses all 8 slots and some uses one in every draw. `cluster_src`: each row holds distinct clusters, none equal to the row's own cluster. Slots at or beyond cluster_count hold valid numbers that are not used. `cluster_count`: some cluster uses all 16 slots and some uses one in every draw.
All inputs are finite; a program needn't handle non-finite values.
Results may differ from a plain program's by a relative error of at most 0.02.
Values may be sent and summed in bfloat16 or wider, within the bound.
A program may use at most 64 MiB of HBM per device.

v0:
```python
import math

import jax
import jax.numpy as jnp
from jax import lax
from jax.sharding import PartitionSpec as P

REACH = 2


softening = 0.0025


def with_halo(cells, sides, width):
    for axis, dim in sides:
        count = lax.axis_size(axis)
        ends = count - 1
        head = lax.slice_in_dim(cells, 0, width, axis=dim)
        tail = lax.slice_in_dim(cells, cells.shape[dim] - width, cells.shape[dim], axis=dim)
        cells = jnp.concatenate(
            [
                lax.ppermute(tail, axis, [(i, (i + 1) % count) for i in range(ends)]),
                cells,
                lax.ppermute(head, axis, [((i + 1) % count, i) for i in range(ends)]),
            ],
            axis=dim,
        )
    return cells


def shards(
    signal,
    points,
    basis,
    transfer,
    leaf_src,
    leaf_count,
    leaf_blocks,
    cluster_src,
    cluster_count,
    cluster_blocks,
):
    leaf_total = basis.shape[0]
    leaf_width = basis.shape[1]
    vector_rows = signal.shape[0]
    signal_leaves = signal.reshape(vector_rows, leaf_total, leaf_width)
    leaf_coefs = jnp.einsum(
        "vln,lnr->lvr", signal_leaves, basis, preferred_element_type=jnp.float32
    ).astype(jnp.bfloat16)
    grouped = lax.all_gather(leaf_coefs, "grp", axis=0, tiled=True)
    partial_up = jnp.einsum("lvr,lrs->vs", leaf_coefs, transfer, preferred_element_type=jnp.float32)
    upward = lax.psum(partial_up.astype(jnp.bfloat16), "grp")
    cluster_coef = upward[None]
    slot_total = cluster_count[0]
    slot_src = cluster_src[0]
    slot_blocks = cluster_blocks[0]
    slot_ids = lax.axis_index("grp") * slot_src.shape[0] + lax.iota(jnp.int32, slot_src.shape[0])
    slot_alive = slot_ids < slot_total
    shards_in = lax.all_gather(cluster_coef, "leaf", axis=0, tiled=True)
    row_ids = lax.iota(jnp.int32, shards_in.shape[0])
    select = ((slot_src[:, None] == row_ids[None, :]) & slot_alive[:, None]).astype(jnp.bfloat16)
    picked = jnp.einsum(
        "sk,kvr->svr", select, shards_in, preferred_element_type=jnp.float32
    ).astype(jnp.bfloat16)
    coupled = jnp.einsum("svr,srt->vt", picked, slot_blocks, preferred_element_type=jnp.float32)
    coupled = lax.psum(coupled.astype(jnp.bfloat16), "grp").astype(jnp.float32)
    cluster_field = coupled.astype(jnp.bfloat16)
    downward_sweep = jnp.einsum(
        "vp,lcp->lvc", cluster_field, transfer, preferred_element_type=jnp.float32
    )
    sources = jnp.take(grouped, leaf_src, axis=0)
    slot_live = lax.iota(jnp.int32, leaf_src.shape[1])[None, :] < leaf_count[:, None]
    sources = jnp.where(slot_live[:, :, None, None], sources, jnp.zeros((), jnp.bfloat16))
    across = jnp.einsum("lkvr,lkrs->lvs", sources, leaf_blocks, preferred_element_type=jnp.float32)
    leaf_field = (downward_sweep + across).astype(jnp.bfloat16)
    stacked = jnp.concatenate([points, signal], axis=0)
    padded = with_halo(stacked, ((("leaf", "grp"), 1),), REACH * leaf_width)
    extent = (2 * REACH + 1) * leaf_width
    kernel_scale = 0.5 / math.sqrt(extent)

    def one_leaf(leaf_index, output):
        first_col = leaf_index * leaf_width
        slice_span = lax.dynamic_slice_in_dim(padded, first_col, extent, 1)
        target = lax.dynamic_slice_in_dim(padded, first_col + REACH * leaf_width, leaf_width, 1)[
            :3
        ].astype(jnp.float32)
        source = slice_span[:3].astype(jnp.float32)
        distance = jnp.zeros((extent, leaf_width), jnp.float32)
        for axis_id in range(3):
            offset = source[axis_id][:, None] - target[axis_id][None, :]
            distance = distance + offset * offset
        kernel = (kernel_scale * lax.rsqrt(distance + softening)).astype(jnp.bfloat16)
        near_part = jnp.dot(slice_span[3:], kernel, preferred_element_type=jnp.float32)
        basis_leaf = lax.dynamic_index_in_dim(basis, leaf_index, 0, keepdims=False)
        field_leaf = lax.dynamic_index_in_dim(leaf_field, leaf_index, 0, keepdims=False)
        far_part = lax.dot_general(
            field_leaf, basis_leaf, (((1,), (1,)), ((), ())), preferred_element_type=jnp.float32
        )
        result_block = (near_part + far_part).astype(jnp.bfloat16)
        return lax.dynamic_update_slice_in_dim(output, result_block, first_col, 1)

    return lax.fori_loop(
        0, leaf_total, one_leaf, jnp.zeros((vector_rows, leaf_total * leaf_width), jnp.bfloat16)
    )


def solution(mesh):
    placed = (
        P(None, ("leaf", "grp")),
        P(None, ("leaf", "grp")),
        P(("leaf", "grp"), None, None),
        P(("leaf", "grp"), None, None),
        P(("leaf", "grp"), None),
        P(("leaf", "grp")),
        P(("leaf", "grp"), None, None, None),
        P("leaf", "grp"),
        P("leaf"),
        P("leaf", "grp", None, None),
    )
    return jax.shard_map(
        shards, mesh=mesh, in_specs=placed, out_specs=P(None, ("leaf", "grp")), check_vma=False
    )
```

profile of v0, /device:TPU:16, one launch (start us, length us, event | category | flops | bytes accessed | tf_op | source)
XLA Modules:
  0.0 216.7 jit_solution(11892481207731103362)
XLA Ops:
  6.5 0.0 copy-start
  6.5 0.0 all-gather.5.cloned.1.call-start
  6.6 2.5 %convolution_convert_fusion = bf16[8,64,128]{2,1,0:T(8,128)(2,1)} fusion(bf16[8,512,128]{2,1,0:T(8,128)(2,1)} %param.14, bf16[8,8,8,512]{3,2,1,0:T(8,128)(2,1)} %bitcast.62), kind=kOutput, calls=%fused_computation.23 | convolution fusion | flops 67174400 | bytes 1703936 | tf_op jit(solution)/shard_map/vln,lnr->lvr/dot_general | solution.py:47
  9.1 0.0 all-gather.5.cloned.1.call-update
  9.1 0.0 all-gather.3.cloned.1.call-start
  9.2 1.2 fusion.15
  10.4 36.6 %psum.14 = bf16[1,64,128]{2,1,0:T(8,128)(2,1)} all-reduce(bf16[1,64,128]{2,1,0:T(8,128)(2,1)S(1)} %fusion.15), channel_id=1, replica_groups=mesh['leaf'=64,'grp'=8] {'grp'}, use_global_device_ids=true, to_apply=%region_0.0 | all-reduce | flops 8192 | bytes 32768 | tf_op jit(solution)/shard_map/psum | solution.py:52
  46.9 0.0 all-gather.3.cloned.1.call-update
  47.0 0.0 copy-done.1
  47.0 0.0 copy-done.4
  47.0 0.1 pad_maximum_fusion.2
  47.1 0.0 copy-start.6
  47.1 1.9 collective-permute-start
  49.0 5.8 %collective-permute-start.1 = (bf16[67,1024]{1,0:T(8,128)(2,1)S(1)}, bf16[67,1024]{1,0:T(8,128)(2,1)}, u32[]{:S(2)}, u32[]{:S(2)}) collective-permute-start(bf16[67,1024]{1,0:T(8,128)(2,1)S(1)} %get-tuple-element.155), channel_id=1, source_target_pairs={{1,0},{2,1},{3,2},{4,3},{5,4},{6,5},{7,6},{8,7},{9,8},{10,9},{11,1... | collective-permute-start | bytes 411656 | tf_op jit(solution)/shard_map/ppermute | solution.py:24
  55.4 0.0 copy-done.5
  55.4 0.0 copy-done.8
  55.4 0.1 iota_compare_fusion
  55.5 0.6 add_compare_fusion
  56.1 0.1 reshape.41
  56.2 0.0 collective-permute-done
  56.2 0.0 copy-start.3
  56.2 0.7 copy-done.3
  56.8 0.6 collective-permute-done.1
  57.4 1.1 pad_maximum_fusion
  58.6 0.0 copy-start.7
  58.6 0.0 copy-start.2
  58.6 0.0 all-gather.5.cloned.1.call-done
  58.6 2.9 %gather_fusion = bf16[64,64,128]{2,1,0:T(8,128)(2,1)} fusion(bf16[64,64,128]{2,1,0:T(8,128)(2,1)} %all-gather.5.cloned.1.call-done, s32[1024]{0:T(1024)S(1)} %pad_clamp_fusion), kind=kCustom, calls=%fused_computation | custom fusion | bytes 2097408 | tf_op jit(solution)/shard_map/jit(_take)/gather | solution.py:71
  61.5 77.6 %all-gather.3.cloned.1.call-done = bf16[64,64,128]{2,1,0:T(8,128)(2,1)} async-done(((bf16[1,64,128]{2,1,0:T(8,128)(2,1)}), bf16[64,64,128]{2,1,0:T(8,128)(2,1)}) %all-gather.3.cloned.1.call-update) | async-done | bytes 1048592 | tf_op jit(solution)/shard_map/all_gather | solution.py:59
  139.2 0.0 copy-done.6
  139.2 0.0 copy-done.7
  139.2 1.9 fusion.16
  141.1 1.0 fusion.14
  142.0 30.9 %psum.15 = bf16[64,128]{1,0:T(8,128)(2,1)S(1)} all-reduce(bf16[64,128]{1,0:T(8,128)(2,1)S(1)} %fusion.14), channel_id=1, replica_groups=mesh['leaf'=64,'grp'=8] {'grp'}, use_global_device_ids=true, to_apply=%region_1.0 | all-reduce | flops 8192 | bytes 32768 | tf_op jit(solution)/shard_map/psum | solution.py:66
  172.9 0.0 copy-done.2
  172.9 0.2 convolution_bitcast_fusion.1
  173.1 0.0 copy-done
  173.1 1.7 fusion.12
  174.9 0.8 broadcast_in_dim.35
  175.7 34.2 %while.15 = (s32[]{:T(128)}, bf16[64,4096]{1,0:T(8,128)(2,1)}, bf16[67,6144]{1,0:T(8,128)(2,1)S(1)}, bf16[8,64,128]{2,1,0:T(8,128)(2,1)S(1)}, bf16[8,512,128]{2,...) while((s32[]{:T(128)}, bf16[64,4096]{1,0:T(8,128)(2,1)}, ...), condition=%wide.region_3.4_spmd, body=%wide.region_2.3_spmd.sunk | while | flops 190653456 | bytes 976146 | solution.py:102
  175.7 0.1 slice_reduce_fusion.4
  175.8 2.4 %fusion.52 = f32[64,512]{1,0:T(8,128)S(1)} fusion(f32[512]{0:T(512)S(1)} %bitcast.65, f32[2560]{0:T(1024)S(1)} %get-tuple-element.196, f32[512]{0:T(512)S(1)} %bitcast.66, f32[2560]{0:T(1024)S(1)} %get-tuple-element.198, f32[512]{0:T(512)S(1)} %bitcast.64, f32[2560]{0:T(1024)S(1)} %get-tuple-element.200, ...), kind=kOutput, calls=%fused_computation.2.clone.1 | convolution fusion | flops 182190080 | bytes 501768 | tf_op jit(solution)/shard_map/while/body/eval_jaxpr/dot_general | solution.py:93
  178.2 1.7 fusion.53
  180.0 0.1 slice_reduce_fusion.4
  180.1 2.4 %fusion.52 = f32[64,512]{1,0:T(8,128)S(1)} fusion(f32[512]{0:T(512)S(1)} %bitcast.65, f32[2560]{0:T(1024)S(1)} %get-tuple-element.196, f32[512]{0:T(512)S(1)} %bitcast.66, f32[2560]{0:T(1024)S(1)} %get-tuple-element.198, f32[512]{0:T(512)S(1)} %bitcast.64, f32[2560]{0:T(1024)S(1)} %get-tuple-element.200, ...), kind=kOutput, calls=%fused_computation.2.clone.1 | convolution fusion | flops 182190080 | bytes 501768 | tf_op jit(solution)/shard_map/while/body/eval_jaxpr/dot_general | solution.py:93
  182.5 1.7 fusion.53
  184.2 0.1 slice_reduce_fusion.4
  184.4 2.4 %fusion.52 = f32[64,512]{1,0:T(8,128)S(1)} fusion(f32[512]{0:T(512)S(1)} %bitcast.65, f32[2560]{0:T(1024)S(1)} %get-tuple-element.196, f32[512]{0:T(512)S(1)} %bitcast.66, f32[2560]{0:T(1024)S(1)} %get-tuple-element.198, f32[512]{0:T(512)S(1)} %bitcast.64, f32[2560]{0:T(1024)S(1)} %get-tuple-element.200, ...), kind=kOutput, calls=%fused_computation.2.clone.1 | convolution fusion | flops 182190080 | bytes 501768 | tf_op jit(solution)/shard_map/while/body/eval_jaxpr/dot_general | solution.py:93
  186.8 1.7 fusion.53
  188.5 0.1 slice_reduce_fusion.4
  188.6 2.4 %fusion.52 = f32[64,512]{1,0:T(8,128)S(1)} fusion(f32[512]{0:T(512)S(1)} %bitcast.65, f32[2560]{0:T(1024)S(1)} %get-tuple-element.196, f32[512]{0:T(512)S(1)} %bitcast.66, f32[2560]{0:T(1024)S(1)} %get-tuple-element.198, f32[512]{0:T(512)S(1)} %bitcast.64, f32[2560]{0:T(1024)S(1)} %get-tuple-element.200, ...), kind=kOutput, calls=%fused_computation.2.clone.1 | convolution fusion | flops 182190080 | bytes 501768 | tf_op jit(solution)/shard_map/while/body/eval_jaxpr/dot_general | solution.py:93
  191.1 1.7 fusion.53
  192.8 0.1 slice_reduce_fusion.4
  192.9 2.4 %fusion.52 = f32[64,512]{1,0:T(8,128)S(1)} fusion(f32[512]{0:T(512)S(1)} %bitcast.65, f32[2560]{0:T(1024)S(1)} %get-tuple-element.196, f32[512]{0:T(512)S(1)} %bitcast.66, f32[2560]{0:T(1024)S(1)} %get-tuple-element.198, f32[512]{0:T(512)S(1)} %bitcast.64, f32[2560]{0:T(1024)S(1)} %get-tuple-element.200, ...), kind=kOutput, calls=%fused_computation.2.clone.1 | convolution fusion | flops 182190080 | bytes 501768 | tf_op jit(solution)/shard_map/while/body/eval_jaxpr/dot_general | solution.py:93
  195.3 1.7 fusion.53
  197.1 0.1 slice_reduce_fusion.4
  197.2 2.4 %fusion.52 = f32[64,512]{1,0:T(8,128)S(1)} fusion(f32[512]{0:T(512)S(1)} %bitcast.65, f32[2560]{0:T(1024)S(1)} %get-tuple-element.196, f32[512]{0:T(512)S(1)} %bitcast.66, f32[2560]{0:T(1024)S(1)} %get-tuple-element.198, f32[512]{0:T(512)S(1)} %bitcast.64, f32[2560]{0:T(1024)S(1)} %get-tuple-element.200, ...), kind=kOutput, calls=%fused_computation.2.clone.1 | convolution fusion | flops 182190080 | bytes 501768 | tf_op jit(solution)/shard_map/while/body/eval_jaxpr/dot_general | solution.py:93
  199.6 1.7 fusion.53
  201.3 0.1 slice_reduce_fusion.4
  201.4 2.4 %fusion.52 = f32[64,512]{1,0:T(8,128)S(1)} fusion(f32[512]{0:T(512)S(1)} %bitcast.65, f32[2560]{0:T(1024)S(1)} %get-tuple-element.196, f32[512]{0:T(512)S(1)} %bitcast.66, f32[2560]{0:T(1024)S(1)} %get-tuple-element.198, f32[512]{0:T(512)S(1)} %bitcast.64, f32[2560]{0:T(1024)S(1)} %get-tuple-element.200, ...), kind=kOutput, calls=%fused_computation.2.clone.1 | convolution fusion | flops 182190080 | bytes 501768 | tf_op jit(solution)/shard_map/while/body/eval_jaxpr/dot_general | solution.py:93
  203.9 1.7 fusion.53
  205.6 0.1 slice_reduce_fusion.4
  205.7 2.4 %fusion.52 = f32[64,512]{1,0:T(8,128)S(1)} fusion(f32[512]{0:T(512)S(1)} %bitcast.65, f32[2560]{0:T(1024)S(1)} %get-tuple-element.196, f32[512]{0:T(512)S(1)} %bitcast.66, f32[2560]{0:T(1024)S(1)} %get-tuple-element.198, f32[512]{0:T(512)S(1)} %bitcast.64, f32[2560]{0:T(1024)S(1)} %get-tuple-element.200, ...), kind=kOutput, calls=%fused_computation.2.clone.1 | convolution fusion | flops 182190080 | bytes 501768 | tf_op jit(solution)/shard_map/while/body/eval_jaxpr/dot_general | solution.py:93
  208.1 1.7 fusion.53
  (30 shorter events, 0.2 us)
Async XLA Ops:
  6.5 166.6 %copy-start = (bf16[8,8,128,128]{3,2,1,0:T(8,128)(2,1)S(1)}, bf16[8,8,128,128]{3,2,1,0:T(8,128)(2,1)}, u32[]{:S(2)}) copy-start(bf16[8,8,128,128]{3,2,1,0:T(8,128)(2,1)} %param.18) | copy-start | bytes 6291460
  6.5 40.4 %copy-start.1 = (bf16[64,4096]{1,0:T(8,128)(2,1)S(1)}, bf16[64,4096]{1,0:T(8,128)(2,1)}, u32[]{:S(2)}) copy-start(bf16[64,4096]{1,0:T(8,128)(2,1)} %param.12) | copy-start | bytes 1572868
  6.5 40.4 %copy-start.4 = (bf16[3,4096]{1,0:T(4,128)(2,1)S(1)}, bf16[3,4096]{1,0:T(4,128)(2,1)}, u32[]{:S(2)}) copy-start(bf16[3,4096]{1,0:T(4,128)(2,1)} %param.13) | copy-start | bytes 73732
  6.5 48.9 %copy-start.5 = (s32[8,8]{1,0:T(8,128)S(1)}, s32[8,8]{1,0:T(8,128)}, u32[]{:S(2)}) copy-start(s32[8,8]{1,0:T(8,128)} %param.16) | copy-start | bytes 772
  6.5 48.9 %copy-start.8 = (s32[8]{0:T(128)S(1)}, s32[8]{0:T(128)}, u32[]{:S(2)}) copy-start(s32[8]{0:T(128)} %param.17) | copy-start | bytes 100
  6.5 52.1 %all-gather.5.cloned.1.call-start = ((), (), s32[]{:S(2)}) async-start(), calls=%async_computation.1 | async-start | bytes 1179648 | tf_op jit(solution)/shard_map/all_gather | solution.py:50
  9.1 130.1 %all-gather.3.cloned.1.call-start = ((), (), s32[]{:S(2)}) async-start(), calls=%async_computation | async-start | bytes 1064960 | tf_op jit(solution)/shard_map/all_gather | solution.py:59
  47.1 92.1 %copy-start.6 = (s32[1,2]{1,0:T(1,128)S(1)}, s32[1,2]{1,0:T(1,128)}, u32[]{:S(2)}) copy-start(s32[1,2]{1,0:T(1,128)} %param.19) | copy-start | bytes 28
  47.1 9.1 %collective-permute-start = (bf16[67,1024]{1,0:T(8,128)(2,1)S(1)}, bf16[67,1024]{1,0:T(8,128)(2,1)S(1)}, u32[]{:S(2)}, u32[]{:S(2)}) collective-permute-start(bf16[67,1024]{1,0:T(8,128)(2,1)S(1)} %get-tuple-element.154), channel_id=1, source_target_pairs={{0,1},{1,2},{2,3},{3,4},{4,5},{5,6},{6,7},{7,8},{8,9},{9,10},{10,1... | collective-permute-start | bytes 411656 | tf_op jit(solution)/shard_map/ppermute | solution.py:22
  49.0 8.4 %collective-permute-start.1 = (bf16[67,1024]{1,0:T(8,128)(2,1)S(1)}, bf16[67,1024]{1,0:T(8,128)(2,1)}, u32[]{:S(2)}, u32[]{:S(2)}) collective-permute-start(bf16[67,1024]{1,0:T(8,128)(2,1)S(1)} %get-tuple-element.155), channel_id=1, source_target_pairs={{1,0},{2,1},{3,2},{4,3},{5,4},{6,5},{7,6},{8,7},{9,8},{10,9},{11,1... | collective-permute-start | bytes 411656 | tf_op jit(solution)/shard_map/ppermute | solution.py:24
  56.2 0.7 copy-start.3
  58.6 80.6 %copy-start.7 = (pred[2]{0:T(512)(128)(4,1)S(1)}, pred[2]{0:T(512)(128)(4,1)}, u32[]{:S(2)}) copy-start(pred[2]{0:T(512)(128)(4,1)} %add_compare_fusion) | copy-start | bytes 10
  58.6 114.3 %copy-start.2 = (bf16[8,128,128]{2,1,0:T(8,128)(2,1)S(1)}, bf16[8,128,128]{2,1,0:T(8,128)(2,1)}, u32[]{:S(2)}) copy-start(bf16[8,128,128]{2,1,0:T(8,128)(2,1)} %param.15) | copy-start | bytes 786436
Sparse Core Ops, SparseCore 0:
  9.5 47.1 all-gather.4
  60.0 79.1 all-gather.2
where the time goes:
time: 217 us
  waiting for transfers between devices  78.3 us (36%)
  blocking collectives  67.4 us (31%)
  matrix products  41.5 us (19%)
  between operations  14.2 us (7%)
  starting transfers between devices  7.75 us (4%)
  local copies, waits for them, and re-layouts  5.23 us (2%)
    all_gather x1, waiting for transfers between devices, shards(): shards_in = lax.all_gather(cluster_coef, 'leaf', axis=0, tiled=True)  77.6 us
    psum x1, blocking collectives, shards(): upward = lax.psum(partial_up.astype(jnp.bfloat16), 'grp')  36.6 us
    psum x1, blocking collectives, shards(): coupled = lax.psum(coupled.astype(jnp.bfloat16), 'grp').astype(jnp.float32)  30.9 us
    dot_general x8, matrix products, one_leaf(): jnp.dot(slice_span[3:], kernel, preferred_element_type=jnp.float32)  19.3 us
    dot_general x8, matrix products, one_leaf(): lax.dot_general(field_leaf, basis_leaf, (((1,), (1,)), ((), ())), preferr...  13.7 us
    ppermute x1, starting transfers between devices, with_halo(): lax.ppermute(head, axis, [((i + 1) % count, i) for i in range(ends)])  5.75 us
  transfers between devices with their start and end apart: 4, of which 2 were waited for; matrix products, arithmetic and copies ran while one was open for 3% of the time, Pallas kernels for 0%

commit v1 on v0

v1 whole, which is shorter than its diff:
```python
import functools
import math

import jax
import jax.numpy as jnp
from jax import lax
from jax.experimental import pallas as pl
from jax.experimental.pallas import tpu as pltpu
from jax.sharding import PartitionSpec as P

BF = jnp.bfloat16
F32 = jnp.float32
MESH = pl.DeviceIdType.MESH
SOFTENING = 0.0025
LOW = 16


def split3(value):
    first = value.astype(BF).astype(F32)
    rest = value - first
    second = rest.astype(BF).astype(F32)
    return first, second, rest - second


def dot(a, b, contract=((1,), (0,))):
    return lax.dot_general(a, b, (contract, ((), ())), preferred_element_type=F32)


def kernel(
    n_leaf,
    n_grp,
    low,
    signal,
    points,
    basis,
    transfer,
    leaf_src,
    leaf_count,
    leaf_blocks,
    cluster_src,
    cluster_count,
    cluster_blocks,
    out,
    sig,
    feat,
    feat_t,
    base,
    trans,
    blocks,
    coefs,
    acc,
    result,
    part_t,
    reduce_in,
    up,
    own_blocks,
    send_blocks,
    all_blocks,
    send_src,
    all_src,
    src_smem,
    part,
    field_in,
    field,
    load_sem,
    halo_send,
    halo_recv,
    ring_send,
    ring_recv,
    block_send,
    block_recv,
    src_send,
    src_recv,
    reduce_send,
    reduce_recv,
    low_send,
    low_recv,
    high_send,
    high_recv,
    fred_send,
    fred_recv,
    fgat_send,
    fgat_recv,
    smem_sem,
    store_sem,
):
    leaf = lax.axis_index("leaf")
    grp = lax.axis_index("grp")
    rows, cols = signal.shape
    leaves, width, rank = basis.shape
    slots = leaf_blocks.shape[1]
    mine = cluster_blocks.shape[0]
    rslice = rank // n_grp
    vslice = rows // n_grp
    high = n_leaf // low
    half = n_grp // 2
    edge = 2 * width
    extent = 5 * width
    my_low = lax.rem(leaf, low)
    my_high = leaf // low
    rank_id = leaf * n_grp + grp
    total = n_leaf * n_grp
    right_id = lax.rem(rank_id + 1, total)
    left_id = lax.rem(rank_id + total - 1, total)
    right = (right_id // n_grp, lax.rem(right_id, n_grp))
    left = (left_id // n_grp, lax.rem(left_id, n_grp))

    def grp_peer(i):
        return (leaf, lax.rem(grp + i, n_grp))

    def grp_from(i):
        return lax.rem(grp + n_grp - i, n_grp)

    def low_peer(i):
        return (my_high * low + lax.rem(my_low + i, low), grp)

    def low_from(i):
        return my_high * low + lax.rem(my_low + low - i, low)

    def high_peer(i):
        return (lax.rem(my_high + i, high) * low + my_low, grp)

    def high_from(i):
        return lax.rem(my_high + high - i, high)

    def each(n, fn):
        def body(i, carry):
            fn(i)
            return carry

        lax.fori_loop(1, n, body, 0)

    barrier = pltpu.get_barrier_semaphore()

    def greet(device):
        pl.semaphore_signal(barrier, inc=1, device_id=device, device_id_type=MESH)

    greet(left)
    greet(right)
    each(n_grp, lambda i: greet(grp_peer(i)))
    each(low, lambda i: greet(low_peer(i)))
    each(high, lambda i: greet(high_peer(i)))

    loads = [
        pltpu.make_async_copy(signal, sig.at[:, pl.ds(edge, cols)], load_sem.at[0]),
        pltpu.make_async_copy(basis, base, load_sem.at[1]),
        pltpu.make_async_copy(cluster_blocks, own_blocks, load_sem.at[2]),
        pltpu.make_async_copy(transfer, trans, load_sem.at[3]),
        pltpu.make_async_copy(leaf_blocks, blocks, load_sem.at[4]),
    ]
    for load in loads:
        load.start()

    pts = points[...].astype(F32)
    norm = pts[0:1] * pts[0:1] + pts[1:2] * pts[1:2] + pts[2:3] * pts[2:3]
    pieces = jnp.concatenate(split3(norm), axis=0)
    ones = jnp.ones((3, cols), F32)
    soft = jnp.concatenate(split3(jnp.full((1, cols), SOFTENING, F32)), axis=0)
    fill = jnp.zeros((4, cols), F32)
    feat[:, edge : edge + cols] = jnp.concatenate(
        [-2.0 * pts, ones, pieces, ones, fill], axis=0
    ).astype(BF)
    feat_t[...] = jnp.concatenate([pts, pieces, ones, soft, fill], axis=0).T.astype(BF)
    acc[...] = jnp.zeros_like(acc)
    src_row = lax.broadcasted_iota(jnp.int32, (8, 128), 0)
    packed_src = jnp.zeros((8, 128), jnp.int32)
    for i in range(mine):
        packed_src = jnp.where(src_row == i, cluster_src[0, i], packed_src)
    send_src[...] = packed_src
    all_src[grp] = packed_src
    loads[2].wait()
    for i in range(mine):
        alive = (grp * mine + i) < cluster_count[0]
        keep = jnp.where(alive, 1.0, 0.0)
        send_blocks[i] = (own_blocks[i].astype(F32) * keep).astype(BF)

    pl.semaphore_wait(barrier, n_grp - 1 + low - 1 + high - 1 + 2)

    def halo_copies():
        return [
            pltpu.make_async_remote_copy(
                signal.at[:, pl.ds(cols - edge, edge)], sig.at[:, pl.ds(0, edge)],
                halo_send.at[0], halo_recv.at[0], device_id=right, device_id_type=MESH),
            pltpu.make_async_remote_copy(
                signal.at[:, pl.ds(0, edge)], sig.at[:, pl.ds(edge + cols, edge)],
                halo_send.at[1], halo_recv.at[1], device_id=left, device_id_type=MESH),
            pltpu.make_async_remote_copy(
                feat.at[:, pl.ds(cols, edge)], feat.at[:, pl.ds(0, edge)],
                halo_send.at[2], halo_recv.at[2], device_id=right, device_id_type=MESH),
            pltpu.make_async_remote_copy(
                feat.at[:, pl.ds(edge, edge)], feat.at[:, pl.ds(edge + cols, edge)],
                halo_send.at[3], halo_recv.at[3], device_id=left, device_id_type=MESH),
        ]

    def block_copy(i, slot):
        target = grp_peer(i)
        return pltpu.make_async_remote_copy(
            send_blocks.at[:, pl.ds(pl.multiple_of(target[1] * rslice, rslice), rslice), :],
            all_blocks.at[pl.ds(slot * mine, mine)],
            block_send.at[i], block_recv.at[i], device_id=target, device_id_type=MESH)

    def src_copy(i, slot):
        return pltpu.make_async_remote_copy(
            send_src, all_src.at[slot], src_send.at[i], src_recv.at[i],
            device_id=grp_peer(i), device_id_type=MESH)

    def reduce_copy(i, slot):
        target = grp_peer(i)
        return pltpu.make_async_remote_copy(
            part_t.at[pl.ds(pl.multiple_of(target[1] * rslice, rslice), rslice), :],
            reduce_in.at[slot], reduce_send.at[i], reduce_recv.at[i],
            device_id=target, device_id_type=MESH)

    def low_copy(i, slot):
        return pltpu.make_async_remote_copy(
            up.at[leaf], up.at[slot], low_send.at[i], low_recv.at[i],
            device_id=low_peer(i), device_id_type=MESH)

    def high_copy(i, slot):
        return pltpu.make_async_remote_copy(
            up.at[pl.ds(my_high * low, low)], up.at[pl.ds(slot * low, low)],
            high_send.at[i], high_recv.at[i], device_id=high_peer(i), device_id_type=MESH)

    def fred_copy(i, slot):
        target = grp_peer(i)
        return pltpu.make_async_remote_copy(
            part.at[pl.ds(pl.multiple_of(target[1] * vslice, vslice), vslice), :],
            field_in.at[slot], fred_send.at[i], fred_recv.at[i],
            device_id=target, device_id_type=MESH)

    def fgat_copy(i, slot):
        return pltpu.make_async_remote_copy(
            field.at[grp], field.at[slot], fgat_send.at[i], fgat_recv.at[i],
            device_id=grp_peer(i), device_id_type=MESH)

    def ring_copy(side, step, slot):
        target = grp_peer(1) if side == 0 else grp_peer(n_grp - 1)
        ref = coefs.at[slot]
        if step == half - 1:
            ref = ref.at[pl.ds(side * (leaves // 2), leaves // 2)]
        return pltpu.make_async_remote_copy(
            ref, ref, ring_send.at[side, step], ring_recv.at[side, step],
            device_id=target, device_id_type=MESH)

    def ring_start(step):
        ring_copy(0, step, lax.rem(grp + n_grp - step, n_grp)).start()
        ring_copy(1, step, lax.rem(grp + step, n_grp)).start()

    def ring_arrive(step):
        ring_copy(0, step, lax.rem(grp + n_grp - step - 1, n_grp)).wait_recv()
        ring_copy(1, step, lax.rem(grp + step + 1, n_grp)).wait_recv()

    for copy in halo_copies():
        copy.start()
    each(n_grp, lambda i: block_copy(i, grp).start())
    each(n_grp, lambda i: src_copy(i, grp).start())
    all_blocks[pl.ds(grp * mine, mine)] = send_blocks[
        :, pl.ds(pl.multiple_of(grp * rslice, rslice), rslice), :]

    loads[0].wait()
    loads[1].wait()

    def one_coef(l, carry):
        first = pl.multiple_of(edge + l * width, width)
        coefs[grp, l] = dot(sig[:, pl.ds(first, width)], base[l]).astype(BF)
        return carry

    lax.fori_loop(0, leaves, one_coef, 0, unroll=2)
    ring_start(0)
    loads[3].wait()
    upward = jnp.zeros((rows, rank), F32)
    for l in range(leaves):
        upward = upward + dot(coefs[grp, l], trans[l])
    part_t[...] = upward.T.astype(BF)
    each(n_grp, lambda i: reduce_copy(i, grp).start())
    reduce_in[grp] = part_t[pl.ds(pl.multiple_of(grp * rslice, rslice), rslice), :]

    def near(a, carry):
        here = pl.multiple_of(a * width, width)
        inner = pl.multiple_of((a - 2) * width, width)
        square = dot(feat_t[pl.ds(inner, width), :], feat[:, pl.ds(here, 3 * width)])
        close = lax.rsqrt(square).astype(BF)
        acc[:, pl.ds(here, 3 * width)] += dot(sig[:, pl.ds(here, width)], close)
        acc[:, pl.ds(here, width)] += dot(
            sig[:, pl.ds(here + width, 2 * width)], close[:, width:], ((1,), (1,)))
        return carry

    lax.fori_loop(2, 4, near, 0)

    each(n_grp, lambda i: reduce_copy(i, grp_from(i)).wait_recv())
    up[leaf] = jnp.sum(reduce_in[...].astype(F32), axis=0).astype(BF)
    each(low, lambda i: low_copy(i, leaf).start())
    ring_arrive(0)
    ring_start(1)

    lax.fori_loop(4, 6, near, 0)

    each(low, lambda i: low_copy(i, low_from(i)).wait_recv())
    each(high, lambda i: high_copy(i, my_high).start())
    each(n_grp, lambda i: src_copy(i, grp_from(i)).wait_recv())
    to_smem = pltpu.make_async_copy(all_src, src_smem, smem_sem)
    to_smem.start()
    if half > 2:
        ring_arrive(1)
        ring_start(2)

    lax.fori_loop(6, 8, near, 0)

    to_smem.wait()
    each(n_grp, lambda i: block_copy(i, grp_from(i)).wait_recv())
    each(high, lambda i: high_copy(i, high_from(i)).wait_recv())
    picked = jnp.concatenate(
        [up[src_smem[k // mine, k % mine, 0]] for k in range(mine * n_grp)], axis=0)
    stacked = jnp.concatenate([all_blocks[k] for k in range(mine * n_grp)], axis=0)
    part[...] = dot(picked, stacked, ((0,), (0,)))
    each(n_grp, lambda i: fred_copy(i, grp).start())
    field_in[grp] = part[pl.ds(pl.multiple_of(grp * vslice, vslice), vslice), :]
    if half > 3:
        ring_arrive(2)
        ring_start(3)

    for copy in halo_copies():
        copy.wait_recv()

    @pl.when(rank_id == 0)
    def _():
        sig[:, 0:edge] = jnp.zeros((rows, edge), BF)

    @pl.when(rank_id == total - 1)
    def _():
        sig[:, edge + cols :] = jnp.zeros((rows, edge), BF)

    lax.fori_loop(8, 2 + leaves, near, 0)

    each(n_grp, lambda i: fred_copy(i, grp_from(i)).wait_recv())
    field[grp] = jnp.sum(field_in[...], axis=0)
    each(n_grp, lambda i: fgat_copy(i, grp).start())

    square = dot(feat_t[0 : 2 * width, :], feat[:, 0:edge])
    close = lax.rsqrt(square).astype(BF)
    acc[:, edge : edge + width] += dot(sig[:, 0:edge], close[:width], ((1,), (1,)))
    acc[:, edge + width : edge + 2 * width] += dot(
        sig[:, width:edge], close[width:, width:], ((1,), (1,)))

    loads[4].wait()
    ring_arrive(half - 1)

    each(n_grp, lambda i: fgat_copy(i, grp_from(i)).wait_recv())
    top = field[...].reshape(rows, rank).astype(BF)
    scale = 0.5 / math.sqrt(extent)

    def finish(l, carry):
        tiles = []
        for k in range(slots):
            src = leaf_src[l, k]
            tile = coefs[src // leaves, lax.rem(src, leaves)]
            tiles.append(jnp.where(k < leaf_count[l], tile, jnp.zeros_like(tile)))
        weights = blocks[l].reshape(slots * rank, rank)
        total_field = dot(jnp.concatenate(tiles, axis=1), weights)
        total_field = (total_field + dot(top, trans[l], ((1,), (1,)))).astype(BF)
        first = pl.multiple_of(l * width, width)
        near_part = acc[:, pl.ds(pl.multiple_of(edge + l * width, width), width)]
        far_part = dot(total_field, base[l], ((1,), (1,)))
        result[:, pl.ds(first, width)] = (near_part * scale + far_part).astype(BF)
        return carry

    lax.fori_loop(0, leaves, finish, 0)
    store = pltpu.make_async_copy(result, out, store_sem)
    store.start()

    for copy in halo_copies():
        copy.wait_send()
    for step in range(half):
        ring_copy(0, step, lax.rem(grp + n_grp - step, n_grp)).wait_send()
        ring_copy(1, step, lax.rem(grp + step, n_grp)).wait_send()

    def drain(i):
        block_copy(i, grp).wait_send()
        src_copy(i, grp).wait_send()
        reduce_copy(i, grp).wait_send()
        fred_copy(i, grp).wait_send()
        fgat_copy(i, grp).wait_send()

    each(n_grp, drain)
    each(low, lambda i: low_copy(i, leaf).wait_send())
    each(high, lambda i: high_copy(i, my_high).wait_send())
    store.wait()


def shards(n_leaf, n_grp, low, signal, points, basis, transfer, leaf_src, leaf_count,
           leaf_blocks, cluster_src, cluster_count, cluster_blocks):
    rows, cols = signal.shape
    leaves, width, rank = basis.shape
    mine = cluster_blocks.shape[1]
    slots = leaf_blocks.shape[1]
    rslice = rank // n_grp
    vslice = rows // n_grp
    high = n_leaf // low
    half = n_grp // 2
    ext = cols + 4 * width
    dma = pltpu.SemaphoreType.DMA
    anywhere = pl.BlockSpec(memory_space=pl.ANY)
    vmem = pl.BlockSpec(memory_space=pltpu.VMEM)
    smem = pl.BlockSpec(memory_space=pltpu.SMEM)
    return pl.pallas_call(
        functools.partial(kernel, n_leaf, n_grp, low),
        out_shape=jax.ShapeDtypeStruct((rows, cols), BF),
        in_specs=[anywhere, vmem, anywhere, anywhere, smem, smem, anywhere, smem, smem, anywhere],
        out_specs=anywhere,
        scratch_shapes=[
            pltpu.VMEM((rows, ext), BF),
            pltpu.VMEM((16, ext), BF),
            pltpu.VMEM((cols, 16), BF),
            pltpu.VMEM((leaves, width, rank), BF),
            pltpu.VMEM((leaves, rank, rank), BF),
            pltpu.VMEM((leaves, slots, rank, rank), BF),
            pltpu.VMEM((n_grp, leaves, rows, rank), BF),
            pltpu.VMEM((rows, ext), F32),
            pltpu.VMEM((rows, cols), BF),
            pltpu.VMEM((rank, rows), BF),
            pltpu.VMEM((n_grp, rslice, rows), BF),
            pltpu.VMEM((n_leaf, rslice, rows), BF),
            pltpu.VMEM((mine, rank, rank), BF),
            pltpu.VMEM((mine, rank, rank), BF),
            pltpu.VMEM((mine * n_grp, rslice, rank), BF),
            pltpu.VMEM((8, 128), jnp.int32),
            pltpu.VMEM((n_grp, 8, 128), jnp.int32),
            pltpu.SMEM((n_grp, 8, 128), jnp.int32),
            pltpu.VMEM((rows, rank), F32),
            pltpu.VMEM((n_grp, vslice, rank), F32),
            pltpu.VMEM((n_grp, vslice, rank), F32),
            dma((5,)),
            dma((4,)), dma((4,)),
            dma((2, half)), dma((2, half)),
            dma((n_grp,)), dma((n_grp,)),
            dma((n_grp,)), dma((n_grp,)),
            dma((n_grp,)), dma((n_grp,)),
            dma((low,)), dma((low,)),
            dma((high,)), dma((high,)),
            dma((n_grp,)), dma((n_grp,)),
            dma((n_grp,)), dma((n_grp,)),
            dma, dma,
        ],
        compiler_params=pltpu.CompilerParams(
            collective_id=0, has_side_effects=True, vmem_limit_bytes=48 * 1024 * 1024),
        cost_estimate=pl.CostEstimate(
            flops=2 * rows * cols * 6 * width, bytes_accessed=6 * 1024 * 1024,
            transcendentals=3 * cols * width),
        name="h2_product",
    )(signal, points, basis, transfer, leaf_src, leaf_count, leaf_blocks,
      cluster_src, cluster_count, cluster_blocks[0])


def solution(mesh):
    both = ("leaf", "grp")
    placed = (
        P(None, both),
        P(None, both),
        P(both, None, None),
        P(both, None, None),
        P(both, None),
        P(both),
        P(both, None, None, None),
        P("leaf", "grp"),
        P("leaf"),
        P("leaf", "grp", None, None),
    )
    n_leaf, n_grp = mesh.shape["leaf"], mesh.shape["grp"]
    low = LOW if n_leaf > LOW else n_leaf // 2
    return jax.shard_map(
        functools.partial(shards, n_leaf, n_grp, low),
        mesh=mesh, in_specs=placed, out_specs=P(None, both), check_vma=False)
```

time: 217 us -> 60.9 us (0.28)
  the two profiles are of different devices: /device:TPU:16 before, /device:TPU:1 now
where the time goes in v1:
time: 60.9 us; the launch traced here: 60.5 us
  Pallas kernels  50.6 us (83%)
  local copies, waits for them, and re-layouts  9.19 us (15%)
  between operations  0.68 us (1%)
    pallas_call x1, Pallas kernels, shards(): pl.pallas_call(functools.partial(kernel, n_leaf, n_grp, low), out_shape=j...  50.6 us
    unnamed x19, local copies, waits for them, and re-layouts  9.19 us

profile of v1, /device:TPU:1, one launch (start us, length us, event | category | flops | bytes accessed | tf_op | source)
XLA Modules:
  0.0 60.5 jit_solution(1702249176845607435)
XLA Ops:
  0.7 0.0 copy-start
  0.7 1.6 %copy-done = bf16[8,8,128,128]{3,2,1,0:T(8,128)(2,1)S(1)} copy-done((bf16[8,8,128,128]{3,2,1,0:T(8,128)(2,1)S(1)}, bf16[8,8,128,128]{3,2,1,0:T(8,128)(2,1)}, u32[]{:S(2)}) %copy-start) | copy-done | bytes 2097176
  2.2 0.0 copy-start.1
  2.2 1.2 %copy-done.1 = bf16[8,512,128]{2,1,0:T(8,128)(2,1)S(1)} copy-done((bf16[8,512,128]{2,1,0:T(8,128)(2,1)S(1)}, bf16[8,512,128]{2,1,0:T(8,128)(2,1)}, u32[]{:S(2)}) %copy-start.1) | copy-done | bytes 1048600
  3.5 0.0 copy-start.2
  3.5 1.0 %copy-done.2 = bf16[64,4096]{1,0:T(8,128)(2,1)S(1)} copy-done((bf16[64,4096]{1,0:T(8,128)(2,1)S(1)}, bf16[64,4096]{1,0:T(8,128)(2,1)}, u32[]{:S(2)}) %copy-start.2) | copy-done | bytes 524312
  4.5 0.0 copy-start.3
  4.5 0.9 %copy-done.3 = bf16[8,128,128]{2,1,0:T(8,128)(2,1)S(1)} copy-done((bf16[8,128,128]{2,1,0:T(8,128)(2,1)S(1)}, bf16[8,128,128]{2,1,0:T(8,128)(2,1)}, u32[]{:S(2)}) %copy-start.3) | copy-done | bytes 262168
  5.5 0.0 copy-start.4
  5.5 0.8 %copy-done.4 = bf16[1,2,128,128]{3,2,1,0:T(8,128)(2,1)S(1)} copy-done((bf16[1,2,128,128]{3,2,1,0:T(8,128)(2,1)S(1)}, bf16[1,2,128,128]{3,2,1,0:T(8,128)(2,1)}, u32[]{:S(2)}) %copy-start.4) | copy-done | bytes 65560
  6.3 0.0 copy-start.5
  6.3 0.8 %copy-done.5 = bf16[3,4096]{1,0:T(4,128)(2,1)S(1)} copy-done((bf16[3,4096]{1,0:T(4,128)(2,1)S(1)}, bf16[3,4096]{1,0:T(4,128)(2,1)}, u32[]{:S(2)}) %copy-start.5) | copy-done | bytes 24600
  7.1 0.0 copy-start.6
  7.1 0.7 %copy-done.6 = s32[8,8]{1,0:T(8,128)S(1)} copy-done((s32[8,8]{1,0:T(8,128)S(1)}, s32[8,8]{1,0:T(8,128)}, u32[]{:S(2)}) %copy-start.6) | copy-done | bytes 280
  7.7 0.0 copy-start.7
  7.8 0.7 %copy-done.7 = s32[8]{0:T(128)S(1)} copy-done((s32[8]{0:T(128)S(1)}, s32[8]{0:T(128)}, u32[]{:S(2)}) %copy-start.7) | copy-done | bytes 56
  8.4 0.0 copy-start.8
  8.4 0.7 %copy-done.8 = s32[1,2]{1,0:T(1,128)S(1)} copy-done((s32[1,2]{1,0:T(1,128)S(1)}, s32[1,2]{1,0:T(1,128)}, u32[]{:S(2)}) %copy-start.8) | copy-done | bytes 32
  9.1 50.6 %h2_product.1 = bf16[64,4096]{1,0:T(8,128)(2,1)S(1)} custom-call(bf16[64,4096]{1,0:T(8,128)(2,1)S(1)} %copy-done.2, bf16[3,4096]{1,0:T(4,128)(2,1)S(1)} %copy-done.5, bf16[8,512,128]{2,1,0:T(8,128)(2,1)S(1)} %copy-done.1, bf16[8,128,128]{2,1,0:T(8,128)(2,1)S(1)} %copy-done.3, s32[8,8]{1,0:T(8,128)S(1)} %copy-done.6, s32[8]{0:T(128)S(1)} %copy-done.7, ...), custom_call_target="tpu_custom_call" | custom-call | flops 1610612736 | bytes 6291456 | tf_op jit(solution)/shard_map/h2_product/pallas_call | solution.py:405
  59.7 0.8 %copy.13 = bf16[64,4096]{1,0:T(8,128)(2,1)} copy(bf16[64,4096]{1,0:T(8,128)(2,1)S(1)} %h2_product.1) | data formatting | bytes 1048576
Async XLA Ops:
  0.7 1.6 %copy-start = (bf16[8,8,128,128]{3,2,1,0:T(8,128)(2,1)S(1)}, bf16[8,8,128,128]{3,2,1,0:T(8,128)(2,1)}, u32[]{:S(2)}) copy-start(bf16[8,8,128,128]{3,2,1,0:T(8,128)(2,1)} %leaf_blocks.1) | copy-start | bytes 6291460
  2.2 1.2 %copy-start.1 = (bf16[8,512,128]{2,1,0:T(8,128)(2,1)S(1)}, bf16[8,512,128]{2,1,0:T(8,128)(2,1)}, u32[]{:S(2)}) copy-start(bf16[8,512,128]{2,1,0:T(8,128)(2,1)} %basis.1) | copy-start | bytes 3145732
  3.5 1.0 %copy-start.2 = (bf16[64,4096]{1,0:T(8,128)(2,1)S(1)}, bf16[64,4096]{1,0:T(8,128)(2,1)}, u32[]{:S(2)}) copy-start(bf16[64,4096]{1,0:T(8,128)(2,1)} %signal.1) | copy-start | bytes 1572868
  4.5 0.9 %copy-start.3 = (bf16[8,128,128]{2,1,0:T(8,128)(2,1)S(1)}, bf16[8,128,128]{2,1,0:T(8,128)(2,1)}, u32[]{:S(2)}) copy-start(bf16[8,128,128]{2,1,0:T(8,128)(2,1)} %transfer.1) | copy-start | bytes 786436
  5.5 0.8 %copy-start.4 = (bf16[1,2,128,128]{3,2,1,0:T(8,128)(2,1)S(1)}, bf16[1,2,128,128]{3,2,1,0:T(8,128)(2,1)}, u32[]{:S(2)}) copy-start(bf16[1,2,128,128]{3,2,1,0:T(8,128)(2,1)} %param.19) | copy-start | bytes 196612
  6.3 0.8 %copy-start.5 = (bf16[3,4096]{1,0:T(4,128)(2,1)S(1)}, bf16[3,4096]{1,0:T(4,128)(2,1)}, u32[]{:S(2)}) copy-start(bf16[3,4096]{1,0:T(4,128)(2,1)} %points.1) | copy-start | bytes 73732
  7.1 0.7 %copy-start.6 = (s32[8,8]{1,0:T(8,128)S(1)}, s32[8,8]{1,0:T(8,128)}, u32[]{:S(2)}) copy-start(s32[8,8]{1,0:T(8,128)} %leaf_src.1) | copy-start | bytes 772
  7.7 0.7 %copy-start.7 = (s32[8]{0:T(128)S(1)}, s32[8]{0:T(128)}, u32[]{:S(2)}) copy-start(s32[8]{0:T(128)} %leaf_count.1) | copy-start | bytes 100
  8.4 0.7 %copy-start.8 = (s32[1,2]{1,0:T(1,128)S(1)}, s32[1,2]{1,0:T(1,128)}, u32[]{:S(2)}) copy-start(s32[1,2]{1,0:T(1,128)} %cluster_src.1) | copy-start | bytes 28

commit v2 on v0

v2 whole, which is shorter than its diff:
```python
import functools
import math

import jax
import jax.numpy as jnp
from jax import lax
from jax.experimental import pallas as pl
from jax.experimental.pallas import tpu as pltpu
from jax.sharding import PartitionSpec as P

BF = jnp.bfloat16
F32 = jnp.float32
MESH = pl.DeviceIdType.MESH
SOFTENING = 0.0025


def split3(value):
    first = value.astype(BF).astype(F32)
    rest = value - first
    second = rest.astype(BF).astype(F32)
    return first, second, rest - second


def dot(a, b, contract=((1,), (0,))):
    return lax.dot_general(a, b, (contract, ((), ())), preferred_element_type=F32)
VMEM_LIMIT = 63 * 1024 * 1024


def kernel(
    n_leaf, n_grp, n_x,
    signal, points, basis, transfer, leaf_src, leaf_count, leaf_blocks,
    cluster_src, cluster_count, cluster_blocks,
    out,
    sig, pts_in, feat, feat_t, base, trans, blocks, coefs, acc,
    part_t, reduce_in, pair, up, own_blocks, send_blocks, all_blocks,
    all_src, src_smem, field_in, across,
    load_sem, halo_send, halo_recv, ring_send, ring_recv,
    block_send, block_recv, src_send, src_recv, reduce_send, reduce_recv,
    pair_send, pair_recv, plane_send, plane_recv, field_send, field_recv, smem_sem,
):
    leaf = lax.axis_index("leaf")
    grp = lax.axis_index("grp")
    rows, cols = signal.shape
    leaves, width, rank = basis.shape
    slots = leaf_blocks.shape[1]
    mine = cluster_blocks.shape[0]
    rslice = rank // n_grp
    half = n_grp // 2
    n_y = n_leaf // (2 * n_x)
    chips = n_x * n_y
    edge = 2 * width
    extent = 5 * width
    core = lax.rem(leaf, 2)
    chip_y = lax.rem(leaf // 2, n_y)
    chip_x = leaf // (2 * n_y)
    rank_id = leaf * n_grp + grp
    total = n_leaf * n_grp
    right_id = lax.rem(rank_id + 1, total)
    left_id = lax.rem(rank_id + total - 1, total)
    right = (right_id // n_grp, lax.rem(right_id, n_grp))
    left = (left_id // n_grp, lax.rem(left_id, n_grp))
    other = (leaf + 1 - 2 * core, grp)

    def grp_peer(i):
        return (leaf, lax.rem(grp + i, n_grp))

    def plane_peer(i):
        to_x = lax.rem(chip_x + i // n_y, n_x)
        to_y = lax.rem(chip_y + lax.rem(i, n_y), n_y)
        return ((to_x * n_y + to_y) * 2 + core, grp)

    def each(n, fn):
        def body(i, carry):
            fn(i)
            return carry

        lax.fori_loop(1, n, body, 0)

    def remote(src, dst, send, recv, device):
        return pltpu.make_async_remote_copy(
            src, dst, send, recv, device_id=device, device_id_type=MESH)

    def wait_all(ref, n, sem):
        whole = ref.at[pl.ds(1, n - 1)]
        pltpu.make_async_copy(whole, whole, sem).wait()

    loads = [
        pltpu.make_async_copy(signal, sig.at[:, pl.ds(edge, cols)], load_sem.at[0]),
        pltpu.make_async_copy(basis, base, load_sem.at[1]),
        pltpu.make_async_copy(transfer, trans, load_sem.at[2]),
        pltpu.make_async_copy(points, pts_in, load_sem.at[3]),
        pltpu.make_async_copy(cluster_blocks, own_blocks, load_sem.at[4]),
        pltpu.make_async_copy(leaf_blocks, blocks, load_sem.at[5]),
    ]
    for load in loads[:5]:
        load.start()

    barrier = pltpu.get_barrier_semaphore()

    def greet(device):
        pl.semaphore_signal(barrier, inc=1, device_id=device, device_id_type=MESH)

    each(n_grp, lambda i: greet(grp_peer(i)))
    greet(other)
    greet(left)
    greet(right)
    each(chips, lambda i: greet(plane_peer(i)))

    def halo_copy(i):
        return [
            lambda: remote(signal.at[:, pl.ds(cols - edge, edge)], sig.at[:, pl.ds(0, edge)],
                           halo_send.at[0], halo_recv.at[0], right),
            lambda: remote(signal.at[:, pl.ds(0, edge)], sig.at[:, pl.ds(edge + cols, edge)],
                           halo_send.at[1], halo_recv.at[1], left),
            lambda: remote(feat.at[:, pl.ds(cols, edge)], feat.at[:, pl.ds(0, edge)],
                           halo_send.at[2], halo_recv.at[2], right),
            lambda: remote(feat.at[:, pl.ds(edge, edge)], feat.at[:, pl.ds(edge + cols, edge)],
                           halo_send.at[3], halo_recv.at[3], left),
        ][i]()

    def block_copy(i):
        target = grp_peer(i)
        return remote(
            send_blocks.at[:, pl.ds(pl.multiple_of(target[1] * rslice, rslice), rslice), :],
            all_blocks.at[i], block_send, block_recv, target)

    def src_copy(i):
        return remote(all_src.at[0], all_src.at[i], src_send, src_recv, grp_peer(i))

    def reduce_copy(i):
        target = grp_peer(i)
        return remote(
            part_t.at[pl.ds(pl.multiple_of(target[1] * rslice, rslice), rslice), :],
            reduce_in.at[i], reduce_send, reduce_recv, target)

    def pair_copy():
        return remote(pair.at[0], pair.at[1], pair_send, pair_recv, other)

    def plane_copy(i):
        return remote(up.at[0], up.at[i], plane_send, plane_recv, plane_peer(i))

    def field_copy(i):
        return remote(field_in.at[0], field_in.at[i], field_send, field_recv, grp_peer(i))

    def ring_copy(side, step, chunk, slot):
        target = grp_peer(1) if side == 0 else grp_peer(n_grp - 1)
        ref = coefs.at[slot, pl.ds(chunk * (leaves // 2), leaves // 2)]
        return remote(ref, ref, ring_send.at[side, step, chunk],
                      ring_recv.at[side, step, chunk], target)

    def ring_sides(step, chunk):
        return (0, 1) if step < half - 1 else (chunk,)

    def ring_start(step, chunk):
        for side in ring_sides(step, chunk):
            away = n_grp - step if side == 0 else step
            ring_copy(side, step, chunk, lax.rem(grp + away, n_grp)).start()

    def ring_arrive(step, chunk):
        for side in ring_sides(step, chunk):
            away = n_grp - step - 1 if side == 0 else step + 1
            ring_copy(side, step, chunk, lax.rem(grp + away, n_grp)).wait_recv()

    def ring_sent(step, chunk):
        for side in ring_sides(step, chunk):
            away = n_grp - step if side == 0 else step
            ring_copy(side, step, chunk, lax.rem(grp + away, n_grp)).wait_send()

    def ring_pass(step, chunk):
        if step < half:
            ring_arrive(step - 1, chunk)
            ring_start(step, chunk)

    pl.semaphore_wait(barrier, n_grp - 1 + chips - 1 + 3)
    halo_copy(0).start()
    halo_copy(1).start()

    loads[0].wait()
    loads[1].wait()
    for chunk in range(2):
        for l in range(chunk * leaves // 2, (chunk + 1) * leaves // 2):
            first = edge + l * width
            coefs[grp, l] = dot(sig[:, first : first + width], base[l]).astype(BF)
        ring_start(0, chunk)
    loads[2].wait()
    upward = jnp.zeros((rows, rank), F32)
    for l in range(leaves):
        upward = upward + dot(coefs[grp, l], trans[l])
    part_t[...] = upward.T.astype(BF)
    each(n_grp, lambda i: reduce_copy(i).start())
    reduce_in[0] = part_t[pl.ds(pl.multiple_of(grp * rslice, rslice), rslice), :]
    loads[5].start()

    loads[3].wait()
    pts = pts_in[...].astype(F32)
    norm = pts[0:1] * pts[0:1] + pts[1:2] * pts[1:2] + pts[2:3] * pts[2:3]
    pieces = jnp.concatenate(split3(norm), axis=0)
    ones = jnp.ones((3, cols), F32)
    soft = jnp.concatenate(split3(jnp.full((1, cols), SOFTENING, F32)), axis=0)
    fill = jnp.zeros((4, cols), F32)
    feat[:, edge : edge + cols] = jnp.concatenate(
        [-2.0 * pts, ones, pieces, ones, fill], axis=0).astype(BF)
    halo_copy(2).start()
    halo_copy(3).start()
    feat_t[...] = jnp.concatenate([pts, pieces, ones, soft, fill], axis=0).T.astype(BF)

    src_row = lax.broadcasted_iota(jnp.int32, (8, 128), 0)
    packed_src = jnp.zeros((8, 128), jnp.int32)
    for i in range(mine):
        packed_src = jnp.where(src_row == i, cluster_src[0, i], packed_src)
    all_src[0] = packed_src
    each(n_grp, lambda i: src_copy(i).start())
    loads[4].wait()
    for i in range(mine):
        alive = (grp * mine + i) < cluster_count[0]
        keep = jnp.where(alive, 1.0, 0.0)
        send_blocks[i] = (own_blocks[i].astype(F32) * keep).astype(BF)
    each(n_grp, lambda i: block_copy(i).start())
    all_blocks[0] = send_blocks[:, pl.ds(pl.multiple_of(grp * rslice, rslice), rslice), :]
    acc[...] = jnp.zeros_like(acc)

    def near(a):
        here = pl.multiple_of(a * width, width)
        inner = pl.multiple_of((a - 2) * width, width)
        square = dot(feat_t[pl.ds(inner, width), :], feat[:, pl.ds(here, 3 * width)])
        close = lax.rsqrt(square).astype(BF)
        acc[:, pl.ds(here, 3 * width)] += dot(sig[:, pl.ds(here, width)], close)
        acc[:, pl.ds(here, width)] += dot(
            sig[:, pl.ds(here + width, 2 * width)], close[:, width:], ((1,), (1,)))

    def slice_sum():
        wait_all(reduce_in, n_grp, reduce_recv)
        pair[0] = jnp.sum(reduce_in[...].astype(F32), axis=0).astype(BF)
        pair_copy().start()

    def plane_out():
        pair_copy().wait_recv()
        one, two = pair[0].astype(F32), pair[1].astype(F32)
        low = jnp.where(core == 0, one, two)
        high = jnp.where(core == 0, two, one)
        up[0] = jnp.concatenate([low, high], axis=1).astype(BF)
        each(chips, lambda i: plane_copy(i).start())

    def to_smem():
        return pltpu.make_async_copy(all_src, src_smem, smem_sem)

    def fetch_src():
        wait_all(all_src, n_grp, src_recv)
        to_smem().start()

    def couple():
        to_smem().wait()
        wait_all(all_blocks, n_grp, block_recv)
        wait_all(up, chips, plane_recv)
        tiles = []
        for i in range(n_grp):
            for j in range(mine):
                src = src_smem[i, j, 0]
                from_x = lax.rem(chip_x + n_x - src // (2 * n_y), n_x)
                from_y = lax.rem(chip_y + n_y - lax.rem(src // 2, n_y), n_y)
                tile = up[from_x * n_y + from_y]
                upper = lax.rem(src, 2) == 0
                tiles.append(jnp.where(upper, tile[:, :rows], tile[:, rows:]))
        stacked = jnp.concatenate(
            [all_blocks[i, j] for i in range(n_grp) for j in range(mine)], axis=0)
        field_in[0] = dot(jnp.concatenate(tiles, axis=0), stacked, ((0,), (0,))).astype(BF)
        each(n_grp, lambda i: field_copy(i).start())

    def halo_arrive():
        for i in range(4):
            halo_copy(i).wait_recv()

        @pl.when(rank_id == 0)
        def _():
            sig[:, 0:edge] = jnp.zeros((rows, edge), BF)

        @pl.when(rank_id == total - 1)
        def _():
            sig[:, edge + cols :] = jnp.zeros((rows, edge), BF)

    def events(a):
        if a == 2:
            ring_pass(1, 0)
        if a == 3:
            slice_sum()
            ring_pass(1, 1)
        if a == 4:
            plane_out()
            fetch_src()
        if a == 5:
            ring_pass(2, 0)
        if a == 6:
            ring_pass(2, 1)
        if a == 7:
            halo_arrive()
            ring_pass(3, 0)
        if a == 8:
            ring_pass(3, 1)

    def near_step(a, carry):
        near(a)
        for at in range(2, 9):
            @pl.when(a == at)
            def _():
                events(at)
        return carry

    lax.fori_loop(2, 2 + leaves, near_step, 0)
    couple()
    square = dot(feat_t[0 : 2 * width, :], feat[:, 0:edge])
    close = lax.rsqrt(square).astype(BF)
    acc[:, edge : edge + width] += dot(sig[:, 0:edge], close[:width], ((1,), (1,)))
    acc[:, edge + width : edge + 2 * width] += dot(
        sig[:, width:edge], close[width:, width:], ((1,), (1,)))

    loads[5].wait()
    ring_arrive(half - 1, 0)
    ring_arrive(half - 1, 1)
    for l in range(leaves):
        tiles = []
        for k in range(slots):
            src = leaf_src[l, k]
            tile = coefs[src // leaves, lax.rem(src, leaves)]
            tiles.append(jnp.where(k < leaf_count[l], tile, jnp.zeros_like(tile)))
        weights = blocks[l].reshape(slots * rank, rank)
        across[l] = dot(jnp.concatenate(tiles, axis=1), weights)

    wait_all(field_in, n_grp, field_recv)
    top = jnp.sum(field_in[...].astype(F32), axis=0).astype(BF)
    scale = 0.5 / math.sqrt(extent)
    for l in range(leaves):
        leaf_field = (across[l] + dot(top, trans[l], ((1,), (1,)))).astype(BF)
        near_part = acc[:, edge + l * width : edge + (l + 1) * width]
        far_part = dot(leaf_field, base[l], ((1,), (1,)))
        out[:, l * width : (l + 1) * width] = (near_part * scale + far_part).astype(BF)

    for i in range(4):
        halo_copy(i).wait_send()
    for step in range(half):
        for chunk in range(2):
            ring_sent(step, chunk)
    wait_all(all_blocks, n_grp, block_send)
    wait_all(all_src, n_grp, src_send)
    wait_all(reduce_in, n_grp, reduce_send)
    pair_copy().wait_send()
    wait_all(up, chips, plane_send)
    wait_all(field_in, n_grp, field_send)


def shards(n_leaf, n_grp, n_x, signal, points, basis, transfer, leaf_src, leaf_count,
           leaf_blocks, cluster_src, cluster_count, cluster_blocks):
    rows, cols = signal.shape
    leaves, width, rank = basis.shape
    mine = cluster_blocks.shape[1]
    slots = leaf_blocks.shape[1]
    rslice = rank // n_grp
    half = n_grp // 2
    ext = cols + 4 * width
    dma = pltpu.SemaphoreType.DMA
    hbm = pl.BlockSpec(memory_space=pltpu.HBM)
    vmem = pl.BlockSpec(memory_space=pltpu.VMEM)
    smem = pl.BlockSpec(memory_space=pltpu.SMEM)
    return pl.pallas_call(
        functools.partial(kernel, n_leaf, n_grp, n_x),
        out_shape=jax.ShapeDtypeStruct((rows, cols), BF),
        in_specs=[hbm, hbm, hbm, hbm, smem, smem, hbm, smem, smem, hbm],
        out_specs=vmem,
        scratch_shapes=[
            pltpu.VMEM((rows, ext), BF),
            pltpu.VMEM(points.shape, BF),
            pltpu.VMEM((16, ext), BF),
            pltpu.VMEM((cols, 16), BF),
            pltpu.VMEM((leaves, width, rank), BF),
            pltpu.VMEM((leaves, rank, rank), BF),
            pltpu.VMEM((leaves, slots, rank, rank), BF),
            pltpu.VMEM((n_grp, leaves, rows, rank), BF),
            pltpu.VMEM((rows, ext), F32),
            pltpu.VMEM((rank, rows), BF),
            pltpu.VMEM((n_grp, rslice, rows), BF),
            pltpu.VMEM((2, rslice, rows), BF),
            pltpu.VMEM((n_leaf // 2, rslice, 2 * rows), BF),
            pltpu.VMEM((mine, rank, rank), BF),
            pltpu.VMEM((mine, rank, rank), BF),
            pltpu.VMEM((n_grp, mine, rslice, rank), BF),
            pltpu.VMEM((n_grp, 8, 128), jnp.int32),
            pltpu.SMEM((n_grp, 8, 128), jnp.int32),
            pltpu.VMEM((n_grp, rows, rank), BF),
            pltpu.VMEM((leaves, rows, rank), F32),
            dma((6,)),
            dma((4,)), dma((4,)),
            dma((2, half, 2)), dma((2, half, 2)),
            dma, dma, dma, dma, dma, dma, dma, dma, dma, dma, dma, dma, dma,
        ],
        compiler_params=pltpu.CompilerParams(
            collective_id=0, has_side_effects=True, vmem_limit_bytes=VMEM_LIMIT),
        cost_estimate=pl.CostEstimate(
            flops=2 * rows * cols * 6 * width, bytes_accessed=6 * 1024 * 1024,
            transcendentals=3 * cols * width),
        name="h2_product",
    )(signal, points, basis, transfer, leaf_src, leaf_count, leaf_blocks,
      cluster_src, cluster_count, cluster_blocks[0])


def solution(mesh):
    both = ("leaf", "grp")
    placed = (
        P(None, both),
        P(None, both),
        P(both, None, None),
        P(both, None, None),
        P(both, None),
        P(both),
        P(both, None, None, None),
        P("leaf", "grp"),
        P("leaf"),
        P("leaf", "grp", None, None),
    )
    n_leaf, n_grp = mesh.shape["leaf"], mesh.shape["grp"]
    n_x = 4 if n_leaf == 64 else 2
    return jax.shard_map(
        functools.partial(shards, n_leaf, n_grp, n_x),
        mesh=mesh, in_specs=placed, out_specs=P(None, both), check_vma=False)
```

time: 217 us -> 50 us (0.23)
  the two profiles are of different devices: /device:TPU:16 before, /device:TPU:2 now
where the time goes in v2:
time: 50 us; the launch traced here: 49.8 us
  Pallas kernels  47.3 us (95%)
  local copies, waits for them, and re-layouts  1.87 us (4%)
  between operations  0.66 us (1%)
    pallas_call x1, Pallas kernels, shards(): pl.pallas_call(functools.partial(kernel, n_leaf, n_grp, n_x), out_shape=j...  47.3 us
    unnamed x1, local copies, waits for them, and re-layouts  1.87 us

profile of v2, /device:TPU:2, one launch (start us, length us, event | category | flops | bytes accessed | tf_op | source)
XLA Modules:
  0.0 49.8 jit_solution(16743268633954070153)
XLA Ops:
  0.7 47.3 %h2_product.1 = bf16[64,4096]{1,0:T(8,128)(2,1)} custom-call(bf16[64,4096]{1,0:T(8,128)(2,1)} %signal.1, bf16[3,4096]{1,0:T(4,128)(2,1)} %points.1, bf16[8,512,128]{2,1,0:T(8,128)(2,1)} %basis.1, bf16[8,128,128]{2,1,0:T(8,128)(2,1)} %transfer.1, s32[8,8]{1,0:T(8,128)} %leaf_src.1, s32[8]{0:T(128)} %leaf_count.1, bf16[8,8,128,128]{3,2,1,0:T(8,128)(2,1)} %leaf_blocks.1, ...), custom_call_target="tpu_custom_call" | custom-call | flops 1610612736 | bytes 6291456 | tf_op jit(solution)/shard_map/h2_product/pallas_call | solution.py:363
  47.9 1.9 %copy.13 = bf16[64,4096]{1,0:T(8,128)(2,1)} copy(bf16[64,4096]{1,0:T(8,128)(2,1)} %h2_product.1) | data formatting | bytes 1048576

commit v3 on v2

--- a/solution.py
+++ b/solution.py
@@ -23,14 +23,15 @@
 
 def dot(a, b, contract=((1,), (0,))):
     return lax.dot_general(a, b, (contract, ((), ())), preferred_element_type=F32)
-VMEM_LIMIT = 63 * 1024 * 1024
+VMEM_LIMIT = 48 * 1024 * 1024
 
 
 def kernel(
     n_leaf, n_grp, n_x,
-    signal, points, basis, transfer, leaf_src, leaf_count, leaf_blocks,
-    cluster_src, cluster_count, cluster_blocks,
+    signal, points, basis, transfer, leaf_src_in, leaf_count_in, leaf_blocks,
+    cluster_src_in, cluster_count, cluster_blocks,
     out,
+    leaf_src, leaf_count, cluster_src,
     sig, pts_in, feat, feat_t, base, trans, blocks, coefs, acc,
     part_t, reduce_in, pair, up, own_blocks, send_blocks, all_blocks,
     all_src, src_smem, field_in, across,
@@ -69,12 +70,17 @@
         to_y = lax.rem(chip_y + lax.rem(i, n_y), n_y)
         return ((to_x * n_y + to_y) * 2 + core, grp)
 
-    def each(n, fn):
-        def body(i, carry):
+    def ring_distance(i, n):
+        return min(i % n, n - i % n)
+
+    grp_order = sorted(range(1, n_grp), key=lambda i: -ring_distance(i, n_grp))
+    plane_order = sorted(
+        range(1, chips),
+        key=lambda i: -ring_distance(i // n_y, n_x) - ring_distance(i % n_y, n_y))
+
+    def each(order, fn):
+        for i in order:
             fn(i)
-            return carry
-
-        lax.fori_loop(1, n, body, 0)
 
     def remote(src, dst, send, recv, device):
         return pltpu.make_async_remote_copy(
@@ -91,8 +97,11 @@
         pltpu.make_async_copy(points, pts_in, load_sem.at[3]),
         pltpu.make_async_copy(cluster_blocks, own_blocks, load_sem.at[4]),
         pltpu.make_async_copy(leaf_blocks, blocks, load_sem.at[5]),
+        pltpu.make_async_copy(cluster_src_in, cluster_src, load_sem.at[6]),
+        pltpu.make_async_copy(leaf_src_in, leaf_src, load_sem.at[8]),
+        pltpu.make_async_copy(leaf_count_in, leaf_count, load_sem.at[9]),
     ]
-    for load in loads[:5]:
+    for load in loads[:5] + loads[6:]:
         load.start()
 
     barrier = pltpu.get_barrier_semaphore()
@@ -100,11 +109,11 @@
     def greet(device):
         pl.semaphore_signal(barrier, inc=1, device_id=device, device_id_type=MESH)
 
-    each(n_grp, lambda i: greet(grp_peer(i)))
-    greet(other)
+    each(plane_order, lambda i: greet(plane_peer(i)))
+    each(grp_order, lambda i: greet(grp_peer(i)))
     greet(left)
     greet(right)
-    each(chips, lambda i: greet(plane_peer(i)))
+    greet(other)
 
     def halo_copy(i):
         return [
@@ -171,25 +180,22 @@
             ring_arrive(step - 1, chunk)
             ring_start(step, chunk)
 
-    pl.semaphore_wait(barrier, n_grp - 1 + chips - 1 + 3)
-    halo_copy(0).start()
-    halo_copy(1).start()
-
     loads[0].wait()
     loads[1].wait()
-    for chunk in range(2):
-        for l in range(chunk * leaves // 2, (chunk + 1) * leaves // 2):
-            first = edge + l * width
-            coefs[grp, l] = dot(sig[:, first : first + width], base[l]).astype(BF)
-        ring_start(0, chunk)
+    loads[5].start()
+    for l in range(leaves):
+        first = edge + l * width
+        coefs[grp, l] = dot(sig[:, first : first + width], base[l]).astype(BF)
     loads[2].wait()
     upward = jnp.zeros((rows, rank), F32)
     for l in range(leaves):
         upward = upward + dot(coefs[grp, l], trans[l])
     part_t[...] = upward.T.astype(BF)
-    each(n_grp, lambda i: reduce_copy(i).start())
+    pl.semaphore_wait(barrier, n_grp - 1 + chips - 1 + 3)
+    each(grp_order, lambda i: reduce_copy(i).start())
+    ring_start(0, 0)
+    ring_start(0, 1)
     reduce_in[0] = part_t[pl.ds(pl.multiple_of(grp * rslice, rslice), rslice), :]
-    loads[5].start()
 
     loads[3].wait()
     pts = pts_in[...].astype(F32)
@@ -200,23 +206,24 @@
     fill = jnp.zeros((4, cols), F32)
     feat[:, edge : edge + cols] = jnp.concatenate(
         [-2.0 * pts, ones, pieces, ones, fill], axis=0).astype(BF)
-    halo_copy(2).start()
-    halo_copy(3).start()
     feat_t[...] = jnp.concatenate([pts, pieces, ones, soft, fill], axis=0).T.astype(BF)
 
+    loads[6].wait()
     src_row = lax.broadcasted_iota(jnp.int32, (8, 128), 0)
     packed_src = jnp.zeros((8, 128), jnp.int32)
     for i in range(mine):
         packed_src = jnp.where(src_row == i, cluster_src[0, i], packed_src)
     all_src[0] = packed_src
-    each(n_grp, lambda i: src_copy(i).start())
+    each(grp_order, lambda i: src_copy(i).start())
     loads[4].wait()
     for i in range(mine):
         alive = (grp * mine + i) < cluster_count[0]
         keep = jnp.where(alive, 1.0, 0.0)
         send_blocks[i] = (own_blocks[i].astype(F32) * keep).astype(BF)
-    each(n_grp, lambda i: block_copy(i).start())
+    each(grp_order, lambda i: block_copy(i).start())
     all_blocks[0] = send_blocks[:, pl.ds(pl.multiple_of(grp * rslice, rslice), rslice), :]
+    for i in range(4):
+        halo_copy(i).start()
     acc[...] = jnp.zeros_like(acc)
 
     def near(a):
@@ -239,7 +246,7 @@
         low = jnp.where(core == 0, one, two)
         high = jnp.where(core == 0, two, one)
         up[0] = jnp.concatenate([low, high], axis=1).astype(BF)
-        each(chips, lambda i: plane_copy(i).start())
+        each(plane_order, lambda i: plane_copy(i).start())
 
     def to_smem():
         return pltpu.make_async_copy(all_src, src_smem, smem_sem)
@@ -264,7 +271,7 @@
         stacked = jnp.concatenate(
             [all_blocks[i, j] for i in range(n_grp) for j in range(mine)], axis=0)
         field_in[0] = dot(jnp.concatenate(tiles, axis=0), stacked, ((0,), (0,))).astype(BF)
-        each(n_grp, lambda i: field_copy(i).start())
+        each(grp_order, lambda i: field_copy(i).start())
 
     def halo_arrive():
         for i in range(4):
@@ -314,6 +321,8 @@
         sig[:, width:edge], close[width:, width:], ((1,), (1,)))
 
     loads[5].wait()
+    loads[7].wait()
+    loads[8].wait()
     ring_arrive(half - 1, 0)
     ring_arrive(half - 1, 1)
     for l in range(leaves):
@@ -358,14 +367,21 @@
     ext = cols + 4 * width
     dma = pltpu.SemaphoreType.DMA
     hbm = pl.BlockSpec(memory_space=pltpu.HBM)
+    operands = [pltpu.with_memory_space_constraint(v, pltpu.HBM) for v in (
+        signal, points, basis, transfer, leaf_src, leaf_count, leaf_blocks,
+        cluster_src, cluster_blocks[0])]
+    operands.insert(8, cluster_count)
+    smem = pl.BlockSpec(memory_space=pltpu.SMEM)
     vmem = pl.BlockSpec(memory_space=pltpu.VMEM)
-    smem = pl.BlockSpec(memory_space=pltpu.SMEM)
     return pl.pallas_call(
         functools.partial(kernel, n_leaf, n_grp, n_x),
         out_shape=jax.ShapeDtypeStruct((rows, cols), BF),
-        in_specs=[hbm, hbm, hbm, hbm, smem, smem, hbm, smem, smem, hbm],
+        in_specs=[hbm] * 8 + [smem, hbm],
         out_specs=vmem,
         scratch_shapes=[
+            pltpu.SMEM(leaf_src.shape, jnp.int32),
+            pltpu.SMEM(leaf_count.shape, jnp.int32),
+            pltpu.SMEM(cluster_src.shape, jnp.int32),
             pltpu.VMEM((rows, ext), BF),
             pltpu.VMEM(points.shape, BF),
             pltpu.VMEM((16, ext), BF),
@@ -386,7 +402,7 @@
             pltpu.SMEM((n_grp, 8, 128), jnp.int32),
             pltpu.VMEM((n_grp, rows, rank), BF),
             pltpu.VMEM((leaves, rows, rank), F32),
-            dma((6,)),
+            dma((10,)),
             dma((4,)), dma((4,)),
             dma((2, half, 2)), dma((2, half, 2)),
             dma, dma, dma, dma, dma, dma, dma, dma, dma, dma, dma, dma, dma,
@@ -397,8 +413,7 @@
             flops=2 * rows * cols * 6 * width, bytes_accessed=6 * 1024 * 1024,
             transcendentals=3 * cols * width),
         name="h2_product",
-    )(signal, points, basis, transfer, leaf_src, leaf_count, leaf_blocks,
-      cluster_src, cluster_count, cluster_blocks[0])
+    )(*operands)
 
 
 def solution(mesh):

time: 50 us -> 43.5 us (0.87)
  the two profiles are of different devices: /device:TPU:2 before, /device:TPU:8 now
where the time goes in v3:
time: 43.5 us; the launch traced here: 43.4 us
  Pallas kernels  41.9 us (96%)
  local copies, waits for them, and re-layouts  0.8 us (2%)
  between operations  0.66 us (2%)
    pallas_call x1, Pallas kernels, shards(): pl.pallas_call(functools.partial(kernel, n_leaf, n_grp, n_x), out_shape=j...  41.9 us

profile of v3, /device:TPU:8, one launch (start us, length us, event | category | flops | bytes accessed | tf_op | source)
XLA Modules:
  0.0 43.4 jit_solution(7690665854910586493)
XLA Ops:
  0.7 41.9 %h2_product.1 = bf16[64,4096]{1,0:T(8,128)(2,1)S(1)} custom-call(bf16[64,4096]{1,0:T(8,128)(2,1)} %signal.1, bf16[3,4096]{1,0:T(4,128)(2,1)} %points.1, bf16[8,512,128]{2,1,0:T(8,128)(2,1)} %basis.1, bf16[8,128,128]{2,1,0:T(8,128)(2,1)} %transfer.1, s32[8,8]{1,0:T(8,128)} %leaf_src_in.1, s32[8]{0:T(128)} %leaf_count_in.1, ...), custom_call_target="tpu_custom_call" | custom-call | flops 1610612736 | bytes 6291456 | tf_op jit(solution)/shard_map/h2_product/pallas_call | solution.py:376
  42.6 0.8 %copy.13 = bf16[64,4096]{1,0:T(8,128)(2,1)} copy(bf16[64,4096]{1,0:T(8,128)(2,1)S(1)} %h2_product.1) | data formatting | bytes 1048576

commit v4 on v3

--- a/solution.py
+++ b/solution.py
@@ -32,9 +32,9 @@
     cluster_src_in, cluster_count, cluster_blocks,
     out,
     leaf_src, leaf_count, cluster_src,
-    sig, pts_in, feat, feat_t, base, trans, blocks, coefs, acc,
+    sig, pts_in, pts_halo, feat, feat_t, base, trans, blocks, coefs, acc,
     part_t, reduce_in, pair, up, own_blocks, send_blocks, all_blocks,
-    all_src, src_smem, field_in, across,
+    all_src, src_smem, field_in, down,
     load_sem, halo_send, halo_recv, ring_send, ring_recv,
     block_send, block_recv, src_send, src_recv, reduce_send, reduce_recv,
     pair_send, pair_recv, plane_send, plane_recv, field_send, field_recv, smem_sem,
@@ -121,9 +121,9 @@
                            halo_send.at[0], halo_recv.at[0], right),
             lambda: remote(signal.at[:, pl.ds(0, edge)], sig.at[:, pl.ds(edge + cols, edge)],
                            halo_send.at[1], halo_recv.at[1], left),
-            lambda: remote(feat.at[:, pl.ds(cols, edge)], feat.at[:, pl.ds(0, edge)],
+            lambda: remote(points.at[:, pl.ds(cols - edge, edge)], pts_halo.at[0],
                            halo_send.at[2], halo_recv.at[2], right),
-            lambda: remote(feat.at[:, pl.ds(edge, edge)], feat.at[:, pl.ds(edge + cols, edge)],
+            lambda: remote(points.at[:, pl.ds(0, edge)], pts_halo.at[1],
                            halo_send.at[3], halo_recv.at[3], left),
         ][i]()
 
@@ -197,22 +197,27 @@
     ring_start(0, 1)
     reduce_in[0] = part_t[pl.ds(pl.multiple_of(grp * rslice, rslice), rslice), :]
 
+    def features(cells):
+        pts = cells.astype(F32)
+        n = pts.shape[1]
+        norm = pts[0:1] * pts[0:1] + pts[1:2] * pts[1:2] + pts[2:3] * pts[2:3]
+        pieces = jnp.concatenate(split3(norm), axis=0)
+        ones = jnp.ones((3, n), F32)
+        soft = jnp.concatenate(split3(jnp.full((1, n), SOFTENING, F32)), axis=0)
+        fill = jnp.zeros((4, n), F32)
+        one = jnp.concatenate([-2.0 * pts, ones, pieces, ones, fill], axis=0).astype(BF)
+        return one, jnp.concatenate([pts, pieces, ones, soft, fill], axis=0)
+
     loads[3].wait()
-    pts = pts_in[...].astype(F32)
-    norm = pts[0:1] * pts[0:1] + pts[1:2] * pts[1:2] + pts[2:3] * pts[2:3]
-    pieces = jnp.concatenate(split3(norm), axis=0)
-    ones = jnp.ones((3, cols), F32)
-    soft = jnp.concatenate(split3(jnp.full((1, cols), SOFTENING, F32)), axis=0)
-    fill = jnp.zeros((4, cols), F32)
-    feat[:, edge : edge + cols] = jnp.concatenate(
-        [-2.0 * pts, ones, pieces, ones, fill], axis=0).astype(BF)
-    feat_t[...] = jnp.concatenate([pts, pieces, ones, soft, fill], axis=0).T.astype(BF)
+    here_feat, here_other = features(pts_in[...])
+    feat[:, edge : edge + cols] = here_feat
+    feat_t[...] = here_other.T.astype(BF)
 
     loads[6].wait()
-    src_row = lax.broadcasted_iota(jnp.int32, (8, 128), 0)
-    packed_src = jnp.zeros((8, 128), jnp.int32)
+    src_lane = lax.broadcasted_iota(jnp.int32, (1, 128), 1)
+    packed_src = jnp.zeros((1, 128), jnp.int32)
     for i in range(mine):
-        packed_src = jnp.where(src_row == i, cluster_src[0, i], packed_src)
+        packed_src = jnp.where(src_lane == i, cluster_src[0, i], packed_src)
     all_src[0] = packed_src
     each(grp_order, lambda i: src_copy(i).start())
     loads[4].wait()
@@ -222,9 +227,9 @@
         send_blocks[i] = (own_blocks[i].astype(F32) * keep).astype(BF)
     each(grp_order, lambda i: block_copy(i).start())
     all_blocks[0] = send_blocks[:, pl.ds(pl.multiple_of(grp * rslice, rslice), rslice), :]
-    for i in range(4):
-        halo_copy(i).start()
     acc[...] = jnp.zeros_like(acc)
+    for l in range(leaves):
+        down[l] = dot(base[l], trans[l]).astype(BF)
 
     def near(a):
         here = pl.multiple_of(a * width, width)
@@ -262,7 +267,7 @@
         tiles = []
         for i in range(n_grp):
             for j in range(mine):
-                src = src_smem[i, j, 0]
+                src = src_smem[i, 0, j]
                 from_x = lax.rem(chip_x + n_x - src // (2 * n_y), n_x)
                 from_y = lax.rem(chip_y + n_y - lax.rem(src // 2, n_y), n_y)
                 tile = up[from_x * n_y + from_y]
@@ -276,6 +281,8 @@
     def halo_arrive():
         for i in range(4):
             halo_copy(i).wait_recv()
+        feat[:, 0:edge] = features(pts_halo[0])[0]
+        feat[:, edge + cols :] = features(pts_halo[1])[0]
 
         @pl.when(rank_id == 0)
         def _():
@@ -287,24 +294,29 @@
 
     def events(a):
         if a == 2:
+            slice_sum()
+        if a == 3:
             ring_pass(1, 0)
-        if a == 3:
-            slice_sum()
+            plane_out()
             ring_pass(1, 1)
-        if a == 4:
-            plane_out()
             fetch_src()
+            for i in range(4):
+                halo_copy(i).start()
         if a == 5:
             ring_pass(2, 0)
         if a == 6:
             ring_pass(2, 1)
         if a == 7:
+            couple()
+        if a == 8:
+            ring_pass(3, 0)
+            ring_pass(3, 1)
+
+    def near_step(a, carry):
+        @pl.when(a == leaves)
+        def _():
             halo_arrive()
-            ring_pass(3, 0)
-        if a == 8:
-            ring_pass(3, 1)
-
-    def near_step(a, carry):
+
         near(a)
         for at in range(2, 9):
             @pl.when(a == at)
@@ -313,12 +325,18 @@
         return carry
 
     lax.fori_loop(2, 2 + leaves, near_step, 0)
-    couple()
     square = dot(feat_t[0 : 2 * width, :], feat[:, 0:edge])
     close = lax.rsqrt(square).astype(BF)
     acc[:, edge : edge + width] += dot(sig[:, 0:edge], close[:width], ((1,), (1,)))
     acc[:, edge + width : edge + 2 * width] += dot(
         sig[:, width:edge], close[width:, width:], ((1,), (1,)))
+
+    scale = 0.5 / math.sqrt(extent)
+    wait_all(field_in, n_grp, field_recv)
+    top = jnp.sum(field_in[...].astype(F32), axis=0).astype(BF)
+    for l in range(leaves):
+        cells = pl.ds(edge + l * width, width)
+        acc[:, cells] = acc[:, cells] * scale + dot(top, down[l], ((1,), (1,)))
 
     loads[5].wait()
     loads[7].wait()
@@ -332,16 +350,10 @@
             tile = coefs[src // leaves, lax.rem(src, leaves)]
             tiles.append(jnp.where(k < leaf_count[l], tile, jnp.zeros_like(tile)))
         weights = blocks[l].reshape(slots * rank, rank)
-        across[l] = dot(jnp.concatenate(tiles, axis=1), weights)
-
-    wait_all(field_in, n_grp, field_recv)
-    top = jnp.sum(field_in[...].astype(F32), axis=0).astype(BF)
-    scale = 0.5 / math.sqrt(extent)
-    for l in range(leaves):
-        leaf_field = (across[l] + dot(top, trans[l], ((1,), (1,)))).astype(BF)
+        leaf_field = dot(jnp.concatenate(tiles, axis=1), weights).astype(BF)
+        far_part = dot(leaf_field, base[l], ((1,), (1,)))
         near_part = acc[:, edge + l * width : edge + (l + 1) * width]
-        far_part = dot(leaf_field, base[l], ((1,), (1,)))
-        out[:, l * width : (l + 1) * width] = (near_part * scale + far_part).astype(BF)
+        out[:, l * width : (l + 1) * width] = (near_part + far_part).astype(BF)
 
     for i in range(4):
         halo_copy(i).wait_send()
@@ -384,6 +396,7 @@
             pltpu.SMEM(cluster_src.shape, jnp.int32),
             pltpu.VMEM((rows, ext), BF),
             pltpu.VMEM(points.shape, BF),
+            pltpu.VMEM((2, 3, 2 * width), BF),
             pltpu.VMEM((16, ext), BF),
             pltpu.VMEM((cols, 16), BF),
             pltpu.VMEM((leaves, width, rank), BF),
@@ -398,10 +411,10 @@
             pltpu.VMEM((mine, rank, rank), BF),
             pltpu.VMEM((mine, rank, rank), BF),
             pltpu.VMEM((n_grp, mine, rslice, rank), BF),
-            pltpu.VMEM((n_grp, 8, 128), jnp.int32),
-            pltpu.SMEM((n_grp, 8, 128), jnp.int32),
+            pltpu.VMEM((n_grp, 1, 128), jnp.int32),
+            pltpu.SMEM((n_grp, 1, 128), jnp.int32),
             pltpu.VMEM((n_grp, rows, rank), BF),
-            pltpu.VMEM((leaves, rows, rank), F32),
+            pltpu.VMEM((leaves, width, rank), BF),
             dma((10,)),
             dma((4,)), dma((4,)),
             dma((2, half, 2)), dma((2, half, 2)),

time: 43.5 us -> 40.4 us (0.929)
  Pallas kernels: 41.9 us -> 38.8 us
    pallas_call x1, Pallas kernels: 41.9 us -> 38.8 us  [shards(): pl.pallas_call(functools.partial(kernel, n_leaf, n_grp, n_x), out_shape=j...]
where the time goes in v4:
time: 40.4 us; the launch traced here: 40.3 us
  Pallas kernels  38.8 us (96%)
  local copies, waits for them, and re-layouts  0.8 us (2%)
  between operations  0.66 us (2%)
    pallas_call x1, Pallas kernels, shards(): pl.pallas_call(functools.partial(kernel, n_leaf, n_grp, n_x), out_shape=j...  38.8 us

profile of v4, /device:TPU:8, one launch (start us, length us, event | category | flops | bytes accessed | tf_op | source)
XLA Modules:
  0.0 40.3 jit_solution(12301117840737344636)
XLA Ops:
  0.7 38.8 %h2_product.1 = bf16[64,4096]{1,0:T(8,128)(2,1)S(1)} custom-call(bf16[64,4096]{1,0:T(8,128)(2,1)} %signal.1, bf16[3,4096]{1,0:T(4,128)(2,1)} %points.1, bf16[8,512,128]{2,1,0:T(8,128)(2,1)} %basis.1, bf16[8,128,128]{2,1,0:T(8,128)(2,1)} %transfer.1, s32[8,8]{1,0:T(8,128)} %leaf_src_in.1, s32[8]{0:T(128)} %leaf_count_in.1, ...), custom_call_target="tpu_custom_call" | custom-call | flops 1610612736 | bytes 6291456 | tf_op jit(solution)/shard_map/h2_product/pallas_call | solution.py:388
  39.5 0.8 %copy.13 = bf16[64,4096]{1,0:T(8,128)(2,1)} copy(bf16[64,4096]{1,0:T(8,128)(2,1)S(1)} %h2_product.1) | data formatting | bytes 1048576

commit v5 on v4

--- a/solution.py
+++ b/solution.py
@@ -308,7 +308,6 @@
             ring_pass(2, 1)
         if a == 7:
             couple()
-        if a == 8:
             ring_pass(3, 0)
             ring_pass(3, 1)
 
@@ -318,7 +317,7 @@
             halo_arrive()
 
         near(a)
-        for at in range(2, 9):
+        for at in range(2, 8):
             @pl.when(a == at)
             def _():
                 events(at)

time: 40.4 us -> 41.6 us (1.030)
  Pallas kernels: 38.8 us -> 40 us
    pallas_call x1, Pallas kernels: 38.8 us -> 40 us  [shards(): pl.pallas_call(functools.partial(kernel, n_leaf, n_grp, n_x), out_shape=j...]
where the time goes in v5:
time: 41.6 us; the launch traced here: 41.5 us
  Pallas kernels  40 us (96%)
  local copies, waits for them, and re-layouts  0.8 us (2%)
  between operations  0.66 us (2%)
    pallas_call x1, Pallas kernels, shards(): pl.pallas_call(functools.partial(kernel, n_leaf, n_grp, n_x), out_shape=j...  40 us

profile of v5, /device:TPU:8, one launch (start us, length us, event | category | flops | bytes accessed | tf_op | source)
XLA Modules:
  0.0 41.5 jit_solution(1819783164958535913)
XLA Ops:
  0.7 40.0 %h2_product.1 = bf16[64,4096]{1,0:T(8,128)(2,1)S(1)} custom-call(bf16[64,4096]{1,0:T(8,128)(2,1)} %signal.1, bf16[3,4096]{1,0:T(4,128)(2,1)} %points.1, bf16[8,512,128]{2,1,0:T(8,128)(2,1)} %basis.1, bf16[8,128,128]{2,1,0:T(8,128)(2,1)} %transfer.1, s32[8,8]{1,0:T(8,128)} %leaf_src_in.1, s32[8]{0:T(128)} %leaf_count_in.1, ...), custom_call_target="tpu_custom_call" | custom-call | flops 1610612736 | bytes 6291456 | tf_op jit(solution)/shard_map/h2_product/pallas_call | solution.py:387
  40.7 0.8 %copy.13 = bf16[64,4096]{1,0:T(8,128)(2,1)} copy(bf16[64,4096]{1,0:T(8,128)(2,1)S(1)} %h2_product.1) | data formatting | bytes 1048576
